TPU v7x, 128 devices: a whole 4x4x4 slice. The times are simulated.
128 devices in a mesh: band: 4 (over x_lo, core), slab: 32 (over x_hi, z, y).
Axes of the slice: x: 4 (x_hi: 2, x_lo: 2; x = x_hi * 2 + x_lo), y: 4, z: 4, core: 2. Of those that a mesh axis runs over, the one named last changes fastest.
Arguments:
- resident: float32 [8, 128, 128, 128], P('band', 'slab'), may hold values from -5 to 5
- blocks: float32 [16, 128, 128, 128], P('band', 'slab'), may hold values from -5 to 5
- occupation: float32 [16], replicated, may hold values from 0.25 to 1
Outputs:
- exchange_term: float32 [8, 128, 128, 128], P('band', 'slab')
All inputs are finite; a program needn't handle non-finite values.
Results may differ from a plain program's by a relative error of at most 0.0001.
Values sent between devices are 32-bit elements; how exact they have to be, the bound alone decides.
A program may use at most 128 MiB of HBM per device.

v0:
```python
import math

import jax
import ml_dtypes
import numpy as np
import jax.numpy as jnp
from jax import lax
from jax.experimental import pallas as pl
from jax.experimental.pallas import tpu as pltpu
from jax.sharding import PartitionSpec as P

MESH = pl.DeviceIdType.MESH
PLANES = 4
GRID = 128
ROWS = PLANES * GRID
HALF = ROWS // 2
KAPPA_SQ = 0.01


class Place:
    def __init__(self):
        self.band = lax.axis_index("band")
        slab = lax.axis_index("slab")
        self.core = self.band % 2
        self.half = slab // 16
        self.z = (slab // 4) % 4
        self.y = slab % 4
        self.x = self.half * 2 + self.band // 2

    def device(self, dx=0, dy=0, dz=0, flip=False):
        x, y, z = (self.x + dx) % 4, (self.y + dy) % 4, (self.z + dz) % 4
        core = 1 - self.core if flip else self.core
        return ((x % 2) * 2 + core, (x // 2) * 16 + z * 4 + y)

    def piece(self, half, dy=0, dz=0):
        return half * 16 + ((self.z + dz) % 4) * 4 + (self.y + dy) % 4


class Mail:
    def __init__(self, send_sem, recv_sem):
        self.send_sem, self.recv_sem = send_sem, recv_sem
        self.count = 0
        self.sent = []

    def send(self, src, dst, device):
        number = self.count
        self.count += 1
        copy = pltpu.make_async_remote_copy(
            src_ref=src,
            dst_ref=dst,
            send_sem=self.send_sem.at[number],
            recv_sem=self.recv_sem.at[number],
            device_id=device,
            device_id_type=MESH,
        )
        copy.start()
        self.sent.append(copy)
        return number

    def arrive(self, number, dst, device):
        pltpu.make_async_remote_copy(
            src_ref=dst,
            dst_ref=dst,
            send_sem=self.send_sem.at[number],
            recv_sem=self.recv_sem.at[number],
            device_id=device,
            device_id_type=MESH,
        ).wait_recv()

    def finish(self):
        for copy in self.sent:
            copy.wait_send()


def planes(ref, piece, part=None):
    if part is None:
        return ref.at[pl.ds(piece * ROWS, ROWS)]
    return ref.at[pl.ds(piece * ROWS + part * HALF, HALF)]


def greet(me):
    barrier = pltpu.get_barrier_semaphore()
    near = [me.device(dx=1), me.device(dx=3), me.device(dy=1), me.device(dy=3),
            me.device(dz=1), me.device(dz=3), me.device(dx=2), me.device(flip=True)]
    for other in near:
        pl.semaphore_signal(barrier, inc=1, device_id=other, device_id_type=MESH)
    for k in range(1, 4):
        pl.semaphore_signal(barrier, inc=1, device_id=align_device(me, k), device_id_type=MESH)

    @pl.when(me.band != me.z)
    def _():
        pl.semaphore_signal(barrier, inc=1, device_id=align_device(me, 0), device_id_type=MESH)
        pl.semaphore_wait(barrier, len(near) + 4)

    @pl.when(me.band == me.z)
    def _():
        pl.semaphore_wait(barrier, len(near) + 3)


def align_device(me, step):
    return (me.z, me.half * 16 + me.band * 4 + (me.y + step) % 4)


class Tree:
    def __init__(self, me, mail, full, half, first):
        self.me, self.mail, self.full, self.half = me, mail, full, half
        self.first = first
        self.box = {}

    def off(self, f, s):
        return dict(dy=f % 4, dz=s % 4) if self.first == "y" else dict(dy=s % 4, dz=f % 4)

    def ref(self, f, s, part=None):
        return planes(self.full, self.me.piece(self.half, **self.off(f, s)), part)

    def push(self, key, src, f, s, df, ds, part=None):
        dst = self.ref(f, s, part)
        self.box[key] = self.mail.send(dst if src is None else src, dst, self.me.device(**self.off(df, ds)))

    def take(self, key, f, s, part=None):
        self.mail.arrive(self.box[key], self.ref(f, s, part), self.me.device(**self.off(0, 0)))

    def start(self, src):
        for d in (1, -1):
            self.push(("f", d), src, 0, 0, d, 0)
        for d in (1, -1):
            self.push(("s", 0, d), src, 0, 0, 0, d)

    def row(self):
        for d in (1, -1):
            self.take(("f", d), -d, 0)
            part = 0 if d == 1 else 1
            self.push(("f2", d), None, -d, 0, d, 0, part)
            for e in (1, -1):
                self.push(("s", -d, e), None, -d, 0, 0, e)

    def column(self, f):
        for e in (1, -1):
            self.take(("s", f, e), f, -e)
            part = 0 if e == 1 else 1
            self.push(("s2", f, e), None, f, -e, 0, e, part)

    def far(self):
        for d in (1, -1):
            self.take(("f2", d), 2, 0, 0 if d == 1 else 1)
        for e in (1, -1):
            self.push(("s", 2, e), None, 2, 0, 0, e)

    def last(self, f):
        for e in (1, -1):
            self.take(("s2", f, e), f, 2, 0 if e == 1 else 1)


def split(v):
    high = v.astype(jnp.bfloat16)
    return high, (v - high.astype(jnp.float32)).astype(jnp.bfloat16)


def times(v, table):
    r = jnp.dot(jnp.concatenate(split(v), axis=1), table, preferred_element_type=jnp.float32)
    return r[:, :GRID] + r[:, GRID:]


def under(table, va, vb):
    (ha, la), (hb, lb) = split(va), split(vb)
    values = jnp.concatenate([jnp.concatenate([ha, hb], axis=1), jnp.concatenate([la, lb], axis=1)], axis=0)
    r = jnp.dot(table, values, preferred_element_type=jnp.float32)
    r = r[:GRID] + r[GRID:]
    return r[:, :GRID], r[:, GRID:]


def gather(me, mail, res_ref, blk_ref, rfull, sfull, local_sem, forward):
    send_sem, recv_sem = mail.send_sem, mail.recv_sem
    h = me.half
    mine = me.piece(h)

    def spiece(dx, flip, t):
        x = (me.x + dx) % 4
        core = 1 - me.core if flip else me.core
        return (x // 2) * 16 + ((x % 2) * 2 + core) * 4 + (me.y + t) % 4

    order = (0, 1, 3, 2)
    align_no = {}
    for t in order:
        number = mail.count
        mail.count += 1
        align_no[t] = number
        src = blk_ref.at[(me.y + t) % 4]
        dst = planes(sfull, mine)

        def remote(src=src, dst=dst, t=t, number=number):
            return pltpu.make_async_remote_copy(
                src_ref=src, dst_ref=dst, send_sem=send_sem.at[number], recv_sem=recv_sem.at[number],
                device_id=align_device(me, t), device_id_type=MESH)
        if t:
            copy = remote()
            copy.start()
            mail.sent.append(copy)
        else:
            @pl.when(me.band != me.z)
            def _():
                remote().start()

            @pl.when(me.band == me.z)
            def _():
                pltpu.make_async_copy(src, dst, local_sem.at[1]).start()
            zero = (remote, src, dst)
    swap = mail.send(res_ref.at[1 - h], planes(rfull, mine), me.device(dx=2))
    tree_a = Tree(me, mail, rfull, h, "y")
    tree_b = Tree(me, mail, rfull, 1 - h, "z")
    tree_a.start(res_ref.at[h])
    own = pltpu.make_async_copy(res_ref.at[h], planes(rfull, mine), local_sem.at[0])
    own.start()
    mail.arrive(swap, planes(rfull, me.piece(1 - h)), me.device(dx=2))
    tree_b.start(None)

    xs = {}
    for t in order:
        back = -t % 4
        dst = planes(sfull, spiece(0, False, back))
        if t:
            mail.arrive(align_no[t], dst, align_device(me, back))
        else:
            @pl.when(me.band != me.z)
            def _():
                zero[0]().wait_recv()

            @pl.when(me.band == me.z)
            def _():
                pltpu.make_async_copy(zero[1], zero[2], local_sem.at[1]).wait()
        for d in (1, -1):
            xs[("x", d, back)] = mail.send(dst, dst, me.device(dx=d))
        xs[("c", 0, back)] = mail.send(dst, dst, me.device(flip=True))
    backs = [-t % 4 for t in order]
    tree_a.row()
    tree_b.row()
    tree_a.column(0)
    tree_b.column(0)
    for t in backs:
        for d in (1, -1):
            ref = planes(sfull, spiece(-d, False, t))
            mail.arrive(xs[("x", d, t)], ref, me.device(dx=-d))
            part = 0 if d == 1 else 1
            ref2 = planes(sfull, spiece(-d, False, t), part)
            xs[("x2", d, t)] = mail.send(ref2, ref2, me.device(dx=d))
            xs[("c", -d, t)] = mail.send(ref, ref, me.device(flip=True))
    tree_a.far()
    tree_b.far()
    for d in (-1, 1):
        tree_a.column(d)
        tree_b.column(d)
    for t in backs:
        for d in (1, -1):
            ref2 = planes(sfull, spiece(2, False, t), 0 if d == 1 else 1)
            mail.arrive(xs[("x2", d, t)], ref2, me.device(dx=-d))
        ref = planes(sfull, spiece(2, False, t))
        xs[("c", 2, t)] = mail.send(ref, ref, me.device(flip=True))
    tree_a.column(2)
    tree_b.column(2)
    for f in (0, -1, 1, 2):
        tree_a.last(f)
        tree_b.last(f)
    own.wait()
    for dx in (0, -1, 1, 2):
        forward([spiece(dx, False, t) for t in backs])
    for dx in (0, -1, 1, 2):
        for t in backs:
            mail.arrive(xs[("c", dx, t)], planes(sfull, spiece(dx, True, t)), me.device(flip=True))
        forward([spiece(dx, True, t) for t in backs])

    def finish():
        @pl.when(me.band != me.z)
        def _():
            zero[0]().wait_send()

    return finish


class Sum:
    def __init__(self, me, mail, term, near_s, far_s, near_f, far_f, half, first):
        self.me, self.mail, self.term = me, mail, term
        self.near_s, self.far_s, self.near_f, self.far_f = near_s, far_s, near_f, far_f
        self.half, self.first = half, first
        self.box = {}

    def off(self, f, s):
        return dict(dy=f % 4, dz=s % 4) if self.first == "y" else dict(dy=s % 4, dz=f % 4)

    def ref(self, f, s, part=None):
        return planes(self.term, self.me.piece(self.half, **self.off(f, s)), part)

    def slots(self, d, f=None):
        n = 0 if d == 1 else 1
        if f is None:
            return self.far_f.at[n], self.near_f.at[n]
        return self.far_s.at[f % 4, n], self.near_s.at[f % 4, n]

    def post(self, key, src, dst, df, ds):
        self.box[key] = self.mail.send(src, dst, self.me.device(**self.off(df, ds)))

    def add(self, key, into, slot):
        self.mail.arrive(self.box[key], slot, self.me.device())
        into[...] += slot[...]

    def far_column(self, f):
        for e in (1, -1):
            self.post(("a", f, e), self.ref(f, 2, 0 if e == 1 else 1), self.slots(e, f)[0], 0, e)

    def near_column(self, f):
        for e in (1, -1):
            self.add(("a", f, e), self.ref(f, e, 0 if e == 1 else 1), self.slots(e, f)[0])
            self.post(("b", f, e), self.ref(f, e), self.slots(e, f)[1], 0, e)

    def own_column(self, f):
        for e in (1, -1):
            self.add(("b", f, e), self.ref(f, 0), self.slots(e, f)[1])

    def far_row(self):
        for d in (1, -1):
            self.post(("c", d), self.ref(2, 0, 0 if d == 1 else 1), self.slots(d)[0], d, 0)

    def near_row(self, d):
        self.add(("c", d), self.ref(d, 0, 0 if d == 1 else 1), self.slots(d)[0])
        self.post(("d", d), self.ref(d, 0), self.slots(d)[1], d, 0)

    def own_row(self):
        for d in (1, -1):
            self.add(("d", d), self.ref(0, 0), self.slots(d)[1])


def kernel(res_ref, blk_ref, occ_ref, right_ref, right_t_ref, left_ref, left_t_ref, out_ref,
           rfull, sfull, work, near_s, far_s, near_f, far_f, send_sem, recv_sem, local_sem):
    me = Place()
    greet(me)
    mail = Mail(send_sem, recv_sem)
    h = me.half
    weight = -occ_ref[me.z * 4 + me.y]

    def forward(pieces):
        for piece in pieces:
            @pl.loop(0, PLANES // 2)
            def _(n):
                rows = pl.ds(pl.multiple_of(piece * ROWS + n * 2 * GRID, 2 * GRID), 2 * GRID)
                v = times(rfull[rows, :] * sfull[rows, :], right_ref[...])
                va, vb = under(left_t_ref[...], v[:GRID], v[GRID:])
                work[rows, :] = jnp.concatenate([va, vb], axis=0)

    def backward(pieces):
        for piece in pieces:
            @pl.loop(0, PLANES // 2)
            def _(n):
                start = pl.multiple_of(piece * ROWS + n * 2 * GRID, 2 * GRID)
                rows = pl.ds(start, 2 * GRID)
                va, vb = under(left_ref[...], work[pl.ds(start, GRID), :], work[pl.ds(start + GRID, GRID), :])
                v = times(jnp.concatenate([va, vb], axis=0), right_t_ref[...])
                work[rows, :] = v * (sfull[rows, :] * weight)

    finish = gather(me, mail, res_ref, blk_ref, rfull, sfull, local_sem, forward)

    def wave_sq(index):
        signed = jnp.minimum(index, GRID - index).astype(jnp.float32) * (2.0 * math.pi / GRID)
        return signed * signed

    shape = (GRID, GRID)
    base = wave_sq(lax.broadcasted_iota(jnp.int32, shape, 0)) + wave_sq(lax.broadcasted_iota(jnp.int32, shape, 1)) + KAPPA_SQ

    @pl.loop(0, GRID // 2)
    def _(n):
        ia, ib = pl.ds(2 * n, GRID, stride=GRID), pl.ds(2 * n + 1, GRID, stride=GRID)
        va, vb = under(left_t_ref[...], work[ia, :], work[ib, :])
        va = va * (4.0 * math.pi / (base + wave_sq(2 * n)))
        vb = vb * (4.0 * math.pi / (base + wave_sq(2 * n + 1)))
        va, vb = under(left_ref[...], va, vb)
        work[ia, :] = va
        work[ib, :] = vb

    sums = [
        Sum(me, mail, work, near_s.at[n], far_s.at[n], near_f.at[n], far_f.at[n], half, first)
        for n, (half, first) in enumerate(((1 - h, "z"), (h, "y")))
    ]
    order = (2, 1, -1, 0)

    def pieces(s, f, off):
        return [me.piece(s.half, **s.off(f, off))]

    for f in order:
        for s in sums:
            backward(pieces(s, f, 2))
            s.far_column(f)
    for f in order:
        for s in sums:
            backward(pieces(s, f, 1) + pieces(s, f, -1))
            s.near_column(f)
    for f in order:
        for s in sums:
            backward(pieces(s, f, 0))
    for f in order:
        for s in sums:
            s.own_column(f)
        for s in sums:
            if f == 2:
                s.far_row()
            elif f:
                s.near_row(f)
    for s in sums:
        s.own_row()
    away = planes(work, me.piece(1 - h))
    swap = mail.send(away, out_ref.at[h], me.device(dx=2))
    out_ref[h] = planes(work, me.piece(h))[...]
    mail.arrive(swap, out_ref.at[1 - h], me.device(dx=2))
    mail.finish()
    finish()


MESSAGES = 77 + 41


def basis():
    points = np.arange(GRID)
    freqs = np.minimum(points, GRID - points)
    angles = 2.0 * np.pi * ((points[:, None] * freqs[None, :]) % GRID) / GRID
    table = np.where(points[None, :] > GRID // 2, np.sin(angles), np.cos(angles)) * np.sqrt(2.0 / GRID)
    table[:, 0] /= np.sqrt(2.0)
    table[:, GRID // 2] /= np.sqrt(2.0)
    return table


def tables():
    b = basis()

    def parts(t):
        high = t.astype(ml_dtypes.bfloat16)
        return high, (t - high.astype(np.float64)).astype(ml_dtypes.bfloat16)

    def right(t):
        high, low = parts(t)
        return np.block([[high, low], [high, np.zeros_like(low)]])

    def left(t):
        high, low = parts(t)
        return np.block([[high, high], [low, np.zeros_like(low)]])

    return [jnp.asarray(t) for t in (right(b), right(b.T), left(b), left(b.T))]


def per_device(resident, blocks, occupation):
    vmem = pl.BlockSpec(memory_space=pltpu.VMEM)
    hbm = pl.BlockSpec(memory_space=pl.ANY)
    full = pltpu.VMEM((GRID * GRID, GRID), jnp.float32)
    out = pl.pallas_call(
        kernel,
        out_shape=jax.ShapeDtypeStruct((2, ROWS, GRID), jnp.float32),
        in_specs=[hbm, hbm, pl.BlockSpec(memory_space=pltpu.SMEM)] + [vmem] * 4,
        out_specs=vmem,
        scratch_shapes=[
            full,
            full,
            full,
            pltpu.VMEM((2, 4, 2, ROWS, GRID), jnp.float32),
            pltpu.VMEM((2, 4, 2, HALF, GRID), jnp.float32),
            pltpu.VMEM((2, 2, ROWS, GRID), jnp.float32),
            pltpu.VMEM((2, 2, HALF, GRID), jnp.float32),
            pltpu.SemaphoreType.DMA((MESSAGES,)),
            pltpu.SemaphoreType.DMA((MESSAGES,)),
            pltpu.SemaphoreType.DMA((2,)),
        ],
        compiler_params=pltpu.CompilerParams(
            collective_id=0, has_side_effects=True, vmem_limit_bytes=48 * 2**20
        ),
        cost_estimate=pl.CostEstimate(flops=13 * 10**9, bytes_accessed=10**7, transcendentals=0),
        name="exchange",
    )(
        resident.reshape(2, ROWS, GRID),
        blocks.reshape(4, ROWS, GRID),
        occupation,
        *tables(),
    )
    return out.reshape(2, PLANES, GRID, GRID)


def solution(mesh):
    placed = (P("band", "slab", None, None), P("band", "slab", None, None), P())
    return jax.shard_map(
        per_device,
        mesh=mesh,
        in_specs=placed,
        out_specs=P("band", "slab", None, None),
        check_vma=False,
    )
```

profile of v0, /device:TPU:6, one launch (start us, length us, event | category | flops | bytes accessed | tf_op | source)
XLA Modules:
  0.0 201.6 jit_solution(17180400155233993763)
XLA Ops:
  0.0 0.0 copy-start.2
  0.0 0.7 copy-done.2
  0.7 0.0 copy-start
  0.7 1.2 copy-done
  1.9 0.0 copy-start.1
  1.9 1.0 copy-done.1
  2.9 0.0 copy-start.3
  2.9 0.9 copy-done.3
  3.8 0.0 copy-start.4
  3.8 0.9 copy-done.4
  4.7 0.0 copy-start.5
  4.7 0.9 copy-done.5
  5.6 0.0 copy-start.6
  5.6 0.9 copy-done.6
  6.5 194.3 %exchange.1 = f32[2,512,128]{2,1,0:T(8,128)S(1)} custom-call(f32[2,512,128]{2,1,0:T(8,128)S(1)} %bitcast.5, f32[4,512,128]{2,1,0:T(8,128)S(1)} %bitcast.4, f32[16]{0:T(128)S(1)} %copy-done.2, bf16[256,256]{1,0:T(8,128)(2,1)S(1)} %copy-done.6, bf16[256,256]{1,0:T(8,128)(2,1)S(1)} %copy-done.5, bf16[256,256]{1,0:T(8,128)(2,1)S(1)} %copy-done.4, ...), custom_call_target="tpu_custom_call" | custom-call | flops 12999999488 | bytes 10000000 | tf_op jit(solution)/shard_map/exchange/pallas_call | solution.py:450
  200.8 0.8 copy.9
Async XLA Ops:
  0.0 0.7 copy-start.2
  0.7 1.2 copy-start
  1.9 1.0 copy-start.1
  2.9 0.9 copy-start.3
  3.8 0.9 copy-start.4
  4.7 0.9 copy-start.5
  5.6 0.9 copy-start.6
where the time goes:
time: 203 us; the launch traced here: 202 us
  Pallas kernels  194 us (96%)
  local copies, waits for them, and re-layouts  7.33 us (4%)
    pallas_call x1, Pallas kernels, per_device(): pl.pallas_call(kernel, out_shape=jax.ShapeDtypeStruct((2, ROWS, GRID), jn...  194 us
    unnamed x15, local copies, waits for them, and re-layouts  7.33 us

commit v1 on v0

--- a/solution.py
+++ b/solution.py
@@ -15,6 +15,7 @@
 ROWS = PLANES * GRID
 HALF = ROWS // 2
 KAPPA_SQ = 0.01
+DEEP = 8
 
 
 class Place:
@@ -26,6 +27,7 @@
         self.z = (slab // 4) % 4
         self.y = slab % 4
         self.x = self.half * 2 + self.band // 2
+        self.stays = jnp.logical_and(self.band == self.z, self.core == 0)
 
     def device(self, dx=0, dy=0, dz=0, flip=False):
         x, y, z = (self.x + dx) % 4, (self.y + dy) % 4, (self.z + dz) % 4
@@ -85,20 +87,31 @@
     for other in near:
         pl.semaphore_signal(barrier, inc=1, device_id=other, device_id_type=MESH)
     for k in range(1, 4):
-        pl.semaphore_signal(barrier, inc=1, device_id=align_device(me, k), device_id_type=MESH)
-
-    @pl.when(me.band != me.z)
+        for other in (align_to(me, k), align_from(me, k)):
+            pl.semaphore_signal(barrier, inc=1, device_id=other, device_id_type=MESH)
+
+    @pl.when(jnp.logical_not(me.stays))
     def _():
-        pl.semaphore_signal(barrier, inc=1, device_id=align_device(me, 0), device_id_type=MESH)
-        pl.semaphore_wait(barrier, len(near) + 4)
-
-    @pl.when(me.band == me.z)
+        for other in (align_to(me, 0), align_from(me, 0)):
+            pl.semaphore_signal(barrier, inc=1, device_id=other, device_id_type=MESH)
+        pl.semaphore_wait(barrier, len(near) + 8)
+
+    @pl.when(me.stays)
     def _():
-        pl.semaphore_wait(barrier, len(near) + 3)
-
-
-def align_device(me, step):
-    return (me.z, me.half * 16 + me.band * 4 + (me.y + step) % 4)
+        pl.semaphore_wait(barrier, len(near) + 6)
+
+
+def align_to(me, step):
+    band = ((me.z // 2 + me.core) % 2) * 2 + me.z % 2
+    return (band, me.half * 16 + me.band * 4 + (me.y + step) % 4)
+
+
+def align_z(me, x, core):
+    return ((x + me.z) % 2) * 2 + core
+
+
+def align_from(me, step):
+    return (me.z, me.half * 16 + align_z(me, me.x, me.core) * 4 + (me.y - step) % 4)
 
 
 class Tree:
@@ -177,7 +190,7 @@
     def spiece(dx, flip, t):
         x = (me.x + dx) % 4
         core = 1 - me.core if flip else me.core
-        return (x // 2) * 16 + ((x % 2) * 2 + core) * 4 + (me.y + t) % 4
+        return (x // 2) * 16 + align_z(me, x, core) * 4 + (me.y + t) % 4
 
     order = (0, 1, 3, 2)
     align_no = {}
@@ -191,17 +204,17 @@
         def remote(src=src, dst=dst, t=t, number=number):
             return pltpu.make_async_remote_copy(
                 src_ref=src, dst_ref=dst, send_sem=send_sem.at[number], recv_sem=recv_sem.at[number],
-                device_id=align_device(me, t), device_id_type=MESH)
+                device_id=align_to(me, t), device_id_type=MESH)
         if t:
             copy = remote()
             copy.start()
             mail.sent.append(copy)
         else:
-            @pl.when(me.band != me.z)
+            @pl.when(jnp.logical_not(me.stays))
             def _():
                 remote().start()
 
-            @pl.when(me.band == me.z)
+            @pl.when(me.stays)
             def _():
                 pltpu.make_async_copy(src, dst, local_sem.at[1]).start()
             zero = (remote, src, dst)
@@ -219,13 +232,13 @@
         back = -t % 4
         dst = planes(sfull, spiece(0, False, back))
         if t:
-            mail.arrive(align_no[t], dst, align_device(me, back))
+            mail.arrive(align_no[t], dst, align_from(me, t))
         else:
-            @pl.when(me.band != me.z)
+            @pl.when(jnp.logical_not(me.stays))
             def _():
                 zero[0]().wait_recv()
 
-            @pl.when(me.band == me.z)
+            @pl.when(me.stays)
             def _():
                 pltpu.make_async_copy(zero[1], zero[2], local_sem.at[1]).wait()
         for d in (1, -1):
@@ -269,7 +282,7 @@
         forward([spiece(dx, True, t) for t in backs])
 
     def finish():
-        @pl.when(me.band != me.z)
+        @pl.when(jnp.logical_not(me.stays))
         def _():
             zero[0]().wait_send()
 
@@ -336,24 +349,31 @@
     h = me.half
     weight = -occ_ref[me.z * 4 + me.y]
 
+    def units(pieces, n):
+        return [pl.multiple_of(piece * ROWS + n * 2 * GRID, 2 * GRID) for piece in pieces]
+
     def forward(pieces):
-        for piece in pieces:
-            @pl.loop(0, PLANES // 2)
-            def _(n):
-                rows = pl.ds(pl.multiple_of(piece * ROWS + n * 2 * GRID, 2 * GRID), 2 * GRID)
+        @pl.loop(0, PLANES // 2)
+        def _(n):
+            for start in units(pieces, n):
+                rows = pl.ds(start, 2 * GRID)
                 v = times(rfull[rows, :] * sfull[rows, :], right_ref[...])
                 va, vb = under(left_t_ref[...], v[:GRID], v[GRID:])
-                work[rows, :] = jnp.concatenate([va, vb], axis=0)
+                work[pl.ds(start, GRID), :] = va
+                work[pl.ds(start + GRID, GRID), :] = vb
 
     def backward(pieces):
-        for piece in pieces:
-            @pl.loop(0, PLANES // 2)
-            def _(n):
-                start = pl.multiple_of(piece * ROWS + n * 2 * GRID, 2 * GRID)
-                rows = pl.ds(start, 2 * GRID)
-                va, vb = under(left_ref[...], work[pl.ds(start, GRID), :], work[pl.ds(start + GRID, GRID), :])
+        @pl.loop(0, PLANES // 2)
+        def _(n):
+            starts = units(pieces, n)
+            held = [work[pl.ds(start, 2 * GRID), :] for start in starts]
+            results = []
+            for start, v in zip(starts, held):
+                va, vb = under(left_ref[...], v[:GRID], v[GRID:])
                 v = times(jnp.concatenate([va, vb], axis=0), right_t_ref[...])
-                work[rows, :] = v * (sfull[rows, :] * weight)
+                results.append(v * (sfull[pl.ds(start, 2 * GRID), :] * weight))
+            for start, v in zip(starts, results):
+                work[pl.ds(start, 2 * GRID), :] = v
 
     finish = gather(me, mail, res_ref, blk_ref, rfull, sfull, local_sem, forward)
 
@@ -364,15 +384,18 @@
     shape = (GRID, GRID)
     base = wave_sq(lax.broadcasted_iota(jnp.int32, shape, 0)) + wave_sq(lax.broadcasted_iota(jnp.int32, shape, 1)) + KAPPA_SQ
 
-    @pl.loop(0, GRID // 2)
+    @pl.loop(0, GRID // (2 * DEEP))
     def _(n):
-        ia, ib = pl.ds(2 * n, GRID, stride=GRID), pl.ds(2 * n + 1, GRID, stride=GRID)
-        va, vb = under(left_t_ref[...], work[ia, :], work[ib, :])
-        va = va * (4.0 * math.pi / (base + wave_sq(2 * n)))
-        vb = vb * (4.0 * math.pi / (base + wave_sq(2 * n + 1)))
-        va, vb = under(left_ref[...], va, vb)
-        work[ia, :] = va
-        work[ib, :] = vb
+        indices = [(n * 2 * DEEP + 2 * k, n * 2 * DEEP + 2 * k + 1) for k in range(DEEP)]
+        held = [[work[pl.ds(i, GRID, stride=GRID), :] for i in pair] for pair in indices]
+        results = []
+        for pair, values in zip(indices, held):
+            values = under(left_t_ref[...], *values)
+            values = [v * (4.0 * math.pi / (base + wave_sq(i))) for i, v in zip(pair, values)]
+            results.append(under(left_ref[...], *values))
+        for pair, values in zip(indices, results):
+            for i, v in zip(pair, values):
+                work[pl.ds(i, GRID, stride=GRID), :] = v
 
     sums = [
         Sum(me, mail, work, near_s.at[n], far_s.at[n], near_f.at[n], far_f.at[n], half, first)
@@ -384,16 +407,15 @@
         return [me.piece(s.half, **s.off(f, off))]
 
     for f in order:
+        backward([p for s in sums for p in pieces(s, f, 2)])
         for s in sums:
-            backward(pieces(s, f, 2))
             s.far_column(f)
     for f in order:
+        backward([p for s in sums for e in (1, -1) for p in pieces(s, f, e)])
         for s in sums:
-            backward(pieces(s, f, 1) + pieces(s, f, -1))
             s.near_column(f)
     for f in order:
-        for s in sums:
-            backward(pieces(s, f, 0))
+        backward([p for s in sums for p in pieces(s, f, 0)])
     for f in order:
         for s in sums:
             s.own_column(f)

time: 203 us -> 163 us (0.80)
  the two profiles are of different devices: /device:TPU:6 before, /device:TPU:10 now
where the time goes in v1:
time: 163 us; the launch traced here: 162 us
  Pallas kernels  155 us (95%)
  local copies, waits for them, and re-layouts  7.33 us (4%)
    pallas_call x1, Pallas kernels, per_device(): pl.pallas_call(kernel, out_shape=jax.ShapeDtypeStruct((2, ROWS, GRID), jn...  155 us
    unnamed x15, local copies, waits for them, and re-layouts  7.33 us

profile of v1, /device:TPU:10, one launch (start us, length us, event | category | flops | bytes accessed | tf_op | source)
XLA Modules:
  0.0 162.5 jit_solution(11942606061126433584)
XLA Ops:
  0.0 0.0 copy-start.2
  0.0 0.7 copy-done.2
  0.7 0.0 copy-start
  0.7 1.2 copy-done
  1.9 0.0 copy-start.1
  1.9 1.0 copy-done.1
  2.9 0.0 copy-start.3
  2.9 0.9 copy-done.3
  3.8 0.0 copy-start.4
  3.8 0.9 copy-done.4
  4.7 0.0 copy-start.5
  4.7 0.9 copy-done.5
  5.6 0.0 copy-start.6
  5.6 0.9 copy-done.6
  6.5 155.1 %exchange.1 = f32[2,512,128]{2,1,0:T(8,128)S(1)} custom-call(f32[2,512,128]{2,1,0:T(8,128)S(1)} %bitcast.5, f32[4,512,128]{2,1,0:T(8,128)S(1)} %bitcast.4, f32[16]{0:T(128)S(1)} %copy-done.2, bf16[256,256]{1,0:T(8,128)(2,1)S(1)} %copy-done.6, bf16[256,256]{1,0:T(8,128)(2,1)S(1)} %copy-done.5, bf16[256,256]{1,0:T(8,128)(2,1)S(1)} %copy-done.4, ...), custom_call_target="tpu_custom_call" | custom-call | flops 12999999488 | bytes 10000000 | tf_op jit(solution)/shard_map/exchange/pallas_call | solution.py:472
  161.7 0.8 copy.9
Async XLA Ops:
  0.0 0.7 copy-start.2
  0.7 1.2 copy-start
  1.9 1.0 copy-start.1
  2.9 0.9 copy-start.3
  3.8 0.9 copy-start.4
  4.7 0.9 copy-start.5
  5.6 0.9 copy-start.6

commit v2 on v1

--- a/solution.py
+++ b/solution.py
@@ -15,7 +15,9 @@
 ROWS = PLANES * GRID
 HALF = ROWS // 2
 KAPPA_SQ = 0.01
-DEEP = 8
+STEPS = ('s0', 'row', 'c0', 's1', 'far', 'c1', 's2', 'c2', 'own', 'early', 'last')
+PITCH = GRID + 8
+DEEP = 16
 
 
 class Place:
@@ -228,54 +230,81 @@
     tree_b.start(None)
 
     xs = {}
-    for t in order:
-        back = -t % 4
-        dst = planes(sfull, spiece(0, False, back))
-        if t:
-            mail.arrive(align_no[t], dst, align_from(me, t))
-        else:
-            @pl.when(jnp.logical_not(me.stays))
+    backs = [-t % 4 for t in order]
+    trees = (tree_a, tree_b)
+
+    def collected():
+        for t in order:
+            back = -t % 4
+            dst = planes(sfull, spiece(0, False, back))
+            if t:
+                mail.arrive(align_no[t], dst, align_from(me, t))
+            else:
+                @pl.when(jnp.logical_not(me.stays))
+                def _():
+                    zero[0]().wait_recv()
+
+                @pl.when(me.stays)
+                def _():
+                    pltpu.make_async_copy(zero[1], zero[2], local_sem.at[1]).wait()
+            for d in (1, -1):
+                xs[("x", d, back)] = mail.send(dst, dst, me.device(dx=d))
+            xs[("c", 0, back)] = mail.send(dst, dst, me.device(flip=True))
+
+    def beside():
+        for t in backs:
+            for d in (1, -1):
+                ref = planes(sfull, spiece(-d, False, t))
+                mail.arrive(xs[("x", d, t)], ref, me.device(dx=-d))
+                part = 0 if d == 1 else 1
+                ref2 = planes(sfull, spiece(-d, False, t), part)
+                xs[("x2", d, t)] = mail.send(ref2, ref2, me.device(dx=d))
+                xs[("c", -d, t)] = mail.send(ref, ref, me.device(flip=True))
+
+    def across():
+        for t in backs:
+            for d in (1, -1):
+                ref2 = planes(sfull, spiece(2, False, t), 0 if d == 1 else 1)
+                mail.arrive(xs[("x2", d, t)], ref2, me.device(dx=-d))
+            ref = planes(sfull, spiece(2, False, t))
+            xs[("c", 2, t)] = mail.send(ref, ref, me.device(flip=True))
+
+    def column(*offsets):
+        for f in offsets:
+            for tree in trees:
+                tree.column(f)
+
+    def ready(late):
+        for dx in (0, -1, 1, 2):
+            x = (me.x + dx) % 4
+            same = x // 2 == h
+            close = align_z(me, x, me.core) != (me.z + 2) % 4
+            whole = jnp.logical_and(same, jnp.logical_not(close) if late else close)
+
+            @pl.when(whole)
             def _():
-                zero[0]().wait_recv()
-
-            @pl.when(me.stays)
+                forward([spiece(dx, False, t) for t in range(4)])
+
+            @pl.when(jnp.logical_not(same))
             def _():
-                pltpu.make_async_copy(zero[1], zero[2], local_sem.at[1]).wait()
-        for d in (1, -1):
-            xs[("x", d, back)] = mail.send(dst, dst, me.device(dx=d))
-        xs[("c", 0, back)] = mail.send(dst, dst, me.device(flip=True))
-    backs = [-t % 4 for t in order]
-    tree_a.row()
-    tree_b.row()
-    tree_a.column(0)
-    tree_b.column(0)
-    for t in backs:
-        for d in (1, -1):
-            ref = planes(sfull, spiece(-d, False, t))
-            mail.arrive(xs[("x", d, t)], ref, me.device(dx=-d))
-            part = 0 if d == 1 else 1
-            ref2 = planes(sfull, spiece(-d, False, t), part)
-            xs[("x2", d, t)] = mail.send(ref2, ref2, me.device(dx=d))
-            xs[("c", -d, t)] = mail.send(ref, ref, me.device(flip=True))
-    tree_a.far()
-    tree_b.far()
-    for d in (-1, 1):
-        tree_a.column(d)
-        tree_b.column(d)
-    for t in backs:
-        for d in (1, -1):
-            ref2 = planes(sfull, spiece(2, False, t), 0 if d == 1 else 1)
-            mail.arrive(xs[("x2", d, t)], ref2, me.device(dx=-d))
-        ref = planes(sfull, spiece(2, False, t))
-        xs[("c", 2, t)] = mail.send(ref, ref, me.device(flip=True))
-    tree_a.column(2)
-    tree_b.column(2)
-    for f in (0, -1, 1, 2):
-        tree_a.last(f)
-        tree_b.last(f)
-    own.wait()
-    for dx in (0, -1, 1, 2):
-        forward([spiece(dx, False, t) for t in backs])
+                forward([spiece(dx, False, t) for t in ((2,) if late else (0, 1, 3))])
+
+    steps = {
+        "own": own.wait,
+        "row": lambda: [tree.row() for tree in trees],
+        "far": lambda: [tree.far() for tree in trees],
+        "c0": lambda: column(0),
+        "c1": lambda: column(-1, 1),
+        "c2": lambda: column(2),
+        "last": lambda: [tree.last(f) for f in (0, -1, 1, 2) for tree in trees],
+        "early": lambda: ready(False),
+        "s0": collected,
+        "s1": beside,
+        "s2": across,
+    }
+    for step in STEPS:
+        steps[step]()
+    ready(True)
     for dx in (0, -1, 1, 2):
         for t in backs:
             mail.arrive(xs[("c", dx, t)], planes(sfull, spiece(dx, True, t)), me.device(flip=True))
@@ -342,7 +371,7 @@
 
 
 def kernel(res_ref, blk_ref, occ_ref, right_ref, right_t_ref, left_ref, left_t_ref, out_ref,
-           rfull, sfull, work, near_s, far_s, near_f, far_f, send_sem, recv_sem, local_sem):
+           rfull, sfull, term, work, near_s, far_s, near_f, far_f, send_sem, recv_sem, local_sem):
     me = Place()
     greet(me)
     mail = Mail(send_sem, recv_sem)
@@ -351,6 +380,10 @@
 
     def units(pieces, n):
         return [pl.multiple_of(piece * ROWS + n * 2 * GRID, 2 * GRID) for piece in pieces]
+
+    def pitched(start):
+        first = pl.multiple_of(start // GRID * PITCH, 8)
+        return pl.ds(first, GRID), pl.ds(pl.multiple_of(first + PITCH, 8), GRID)
 
     def forward(pieces):
         @pl.loop(0, PLANES // 2)
@@ -359,21 +392,22 @@
                 rows = pl.ds(start, 2 * GRID)
                 v = times(rfull[rows, :] * sfull[rows, :], right_ref[...])
                 va, vb = under(left_t_ref[...], v[:GRID], v[GRID:])
-                work[pl.ds(start, GRID), :] = va
-                work[pl.ds(start + GRID, GRID), :] = vb
+                one, two = pitched(start)
+                work[one, :] = va
+                work[two, :] = vb
 
     def backward(pieces):
         @pl.loop(0, PLANES // 2)
         def _(n):
             starts = units(pieces, n)
-            held = [work[pl.ds(start, 2 * GRID), :] for start in starts]
+            held = [[work[rows, :] for rows in pitched(start)] for start in starts]
             results = []
-            for start, v in zip(starts, held):
-                va, vb = under(left_ref[...], v[:GRID], v[GRID:])
+            for start, values in zip(starts, held):
+                va, vb = under(left_ref[...], *values)
                 v = times(jnp.concatenate([va, vb], axis=0), right_t_ref[...])
                 results.append(v * (sfull[pl.ds(start, 2 * GRID), :] * weight))
             for start, v in zip(starts, results):
-                work[pl.ds(start, 2 * GRID), :] = v
+                term[pl.ds(start, 2 * GRID), :] = v
 
     finish = gather(me, mail, res_ref, blk_ref, rfull, sfull, local_sem, forward)
 
@@ -387,7 +421,7 @@
     @pl.loop(0, GRID // (2 * DEEP))
     def _(n):
         indices = [(n * 2 * DEEP + 2 * k, n * 2 * DEEP + 2 * k + 1) for k in range(DEEP)]
-        held = [[work[pl.ds(i, GRID, stride=GRID), :] for i in pair] for pair in indices]
+        held = [[work[pl.ds(i, GRID, stride=PITCH), :] for i in pair] for pair in indices]
         results = []
         for pair, values in zip(indices, held):
             values = under(left_t_ref[...], *values)
@@ -395,10 +429,10 @@
             results.append(under(left_ref[...], *values))
         for pair, values in zip(indices, results):
             for i, v in zip(pair, values):
-                work[pl.ds(i, GRID, stride=GRID), :] = v
+                work[pl.ds(i, GRID, stride=PITCH), :] = v
 
     sums = [
-        Sum(me, mail, work, near_s.at[n], far_s.at[n], near_f.at[n], far_f.at[n], half, first)
+        Sum(me, mail, term, near_s.at[n], far_s.at[n], near_f.at[n], far_f.at[n], half, first)
         for n, (half, first) in enumerate(((1 - h, "z"), (h, "y")))
     ]
     order = (2, 1, -1, 0)
@@ -424,13 +458,12 @@
                 s.far_row()
             elif f:
                 s.near_row(f)
-    for s in sums:
-        s.own_row()
-    away = planes(work, me.piece(1 - h))
-    swap = mail.send(away, out_ref.at[h], me.device(dx=2))
-    out_ref[h] = planes(work, me.piece(h))[...]
+    sums[0].own_row()
+    swap = mail.send(planes(term, me.piece(1 - h)), out_ref.at[h], me.device(dx=2))
+    sums[1].own_row()
     mail.arrive(swap, out_ref.at[1 - h], me.device(dx=2))
     mail.finish()
+    out_ref[h] = planes(term, me.piece(h))[...]
     finish()
 
 
@@ -478,6 +511,7 @@
             full,
             full,
             full,
+            pltpu.VMEM((GRID * PITCH, GRID), jnp.float32),
             pltpu.VMEM((2, 4, 2, ROWS, GRID), jnp.float32),
             pltpu.VMEM((2, 4, 2, HALF, GRID), jnp.float32),
             pltpu.VMEM((2, 2, ROWS, GRID), jnp.float32),
@@ -487,7 +521,7 @@
             pltpu.SemaphoreType.DMA((2,)),
         ],
         compiler_params=pltpu.CompilerParams(
-            collective_id=0, has_side_effects=True, vmem_limit_bytes=48 * 2**20
+            collective_id=0, has_side_effects=True, vmem_limit_bytes=56 * 2**20
         ),
         cost_estimate=pl.CostEstimate(flops=13 * 10**9, bytes_accessed=10**7, transcendentals=0),
         name="exchange",

time: 163 us -> 148 us (0.908)
  the two profiles are of different devices: /device:TPU:10 before, /device:TPU:6 now
where the time goes in v2:
time: 148 us; the launch traced here: 146 us
  Pallas kernels  144 us (97%)
  local copies, waits for them, and re-layouts  1.87 us (1%)
    pallas_call x1, Pallas kernels, per_device(): pl.pallas_call(kernel, out_shape=jax.ShapeDtypeStruct((2, ROWS, GRID), jn...  144 us

profile of v2, /device:TPU:6, one launch (start us, length us, event | category | flops | bytes accessed | tf_op | source)
XLA Modules:
  0.0 146.2 jit_solution(14732488722901218262)
XLA Ops:
  0.0 144.3 %exchange.1 = f32[2,512,128]{2,1,0:T(8,128)} custom-call(f32[2,512,128]{2,1,0:T(8,128)} %bitcast.5, f32[4,512,128]{2,1,0:T(8,128)} %bitcast.4, f32[16]{0:T(128)} %occ_ref.1, bf16[256,256]{1,0:T(8,128)(2,1)} %constant.8.clone.right_ref, bf16[256,256]{1,0:T(8,128)(2,1)} %constant.9.clone.right_t_ref, bf16[256,256]{1,0:T(8,128)(2,1)} %constant.10.clone.left_ref, ...), custom_call_target="tpu_custom_call" | custom-call | flops 12999999488 | bytes 10000000 | tf_op jit(solution)/shard_map/exchange/pallas_call | solution.py:505
  144.3 1.9 %copy.9 = f32[2,4,128,128]{3,2,1,0:T(8,128)} copy(f32[2,4,128,128]{3,2,1,0:T(8,128)} %bitcast.3) | data formatting | bytes 1048576

commit v3 on v2

--- a/solution.py
+++ b/solution.py
@@ -29,7 +29,7 @@
         self.z = (slab // 4) % 4
         self.y = slab % 4
         self.x = self.half * 2 + self.band // 2
-        self.stays = jnp.logical_and(self.band == self.z, self.core == 0)
+        self.stays = jnp.logical_and(self.band == 0, self.z == 0)
 
     def device(self, dx=0, dy=0, dz=0, flip=False):
         x, y, z = (self.x + dx) % 4, (self.y + dy) % 4, (self.z + dz) % 4
@@ -104,12 +104,12 @@
 
 
 def align_to(me, step):
-    band = ((me.z // 2 + me.core) % 2) * 2 + me.z % 2
+    band = ((me.band + me.z) % 2) * 2 + me.z // 2
     return (band, me.half * 16 + me.band * 4 + (me.y + step) % 4)
 
 
 def align_z(me, x, core):
-    return ((x + me.z) % 2) * 2 + core
+    return core * 2 + (x + me.z) % 2
 
 
 def align_from(me, step):
@@ -444,13 +444,13 @@
         backward([p for s in sums for p in pieces(s, f, 2)])
         for s in sums:
             s.far_column(f)
-    for f in order:
+    def near(f):
         backward([p for s in sums for e in (1, -1) for p in pieces(s, f, e)])
         for s in sums:
             s.near_column(f)
-    for f in order:
+
+    def own(f):
         backward([p for s in sums for p in pieces(s, f, 0)])
-    for f in order:
         for s in sums:
             s.own_column(f)
         for s in sums:
@@ -458,6 +458,9 @@
                 s.far_row()
             elif f:
                 s.near_row(f)
+
+    for step, f in ((near, 2), (near, 1), (near, -1), (own, 2), (near, 0), (own, 1), (own, -1), (own, 0)):
+        step(f)
     sums[0].own_row()
     swap = mail.send(planes(term, me.piece(1 - h)), out_ref.at[h], me.device(dx=2))
     sums[1].own_row()

time: 148 us -> 142 us (0.959)
  Pallas kernels: 144 us -> 138 us
    pallas_call x1, Pallas kernels: 144 us -> 138 us  [per_device(): pl.pallas_call(kernel, out_shape=jax.ShapeDtypeStruct((2, ROWS, GRID), jn...]
where the time goes in v3:
time: 142 us; the launch traced here: 140 us
  Pallas kernels  138 us (97%)
  local copies, waits for them, and re-layouts  1.87 us (1%)
    pallas_call x1, Pallas kernels, per_device(): pl.pallas_call(kernel, out_shape=jax.ShapeDtypeStruct((2, ROWS, GRID), jn...  138 us

profile of v3, /device:TPU:6, one launch (start us, length us, event | category | flops | bytes accessed | tf_op | source)
XLA Modules:
  0.0 139.8 jit_solution(18013314543943226077)
XLA Ops:
  0.0 138.0 %exchange.1 = f32[2,512,128]{2,1,0:T(8,128)} custom-call(f32[2,512,128]{2,1,0:T(8,128)} %bitcast.5, f32[4,512,128]{2,1,0:T(8,128)} %bitcast.4, f32[16]{0:T(128)} %occ_ref.1, bf16[256,256]{1,0:T(8,128)(2,1)} %constant.8.clone.right_ref, bf16[256,256]{1,0:T(8,128)(2,1)} %constant.9.clone.right_t_ref, bf16[256,256]{1,0:T(8,128)(2,1)} %constant.10.clone.left_ref, ...), custom_call_target="tpu_custom_call" | custom-call | flops 12999999488 | bytes 10000000 | tf_op jit(solution)/shard_map/exchange/pallas_call | solution.py:508
  138.0 1.9 %copy.9 = f32[2,4,128,128]{3,2,1,0:T(8,128)} copy(f32[2,4,128,128]{3,2,1,0:T(8,128)} %bitcast.3) | data formatting | bytes 1048576

commit v4 on v3

--- a/solution.py
+++ b/solution.py
@@ -184,7 +184,7 @@
     return r[:, :GRID], r[:, GRID:]
 
 
-def gather(me, mail, res_ref, blk_ref, rfull, sfull, local_sem, forward):
+def gather(me, mail, res_ref, blk_ref, rfull, sfull, local_sem, fetches, forward):
     send_sem, recv_sem = mail.send_sem, mail.recv_sem
     h = me.half
     mine = me.piece(h)
@@ -290,7 +290,7 @@
                 forward([spiece(dx, False, t) for t in ((2,) if late else (0, 1, 3))])
 
     steps = {
-        "own": own.wait,
+        "own": lambda: [copy.wait() for copy in (own, *fetches)],
         "row": lambda: [tree.row() for tree in trees],
         "far": lambda: [tree.far() for tree in trees],
         "c0": lambda: column(0),
@@ -370,9 +370,15 @@
             self.add(("d", d), self.ref(0, 0), self.slots(d)[1])
 
 
-def kernel(res_ref, blk_ref, occ_ref, right_ref, right_t_ref, left_ref, left_t_ref, out_ref,
+def kernel(res_ref, blk_ref, occ_ref, tables_ref, out_ref, right_ref, right_t_ref, left_ref, left_t_ref,
            rfull, sfull, term, work, near_s, far_s, near_f, far_f, send_sem, recv_sem, local_sem):
     me = Place()
+    fetches = [
+        pltpu.make_async_copy(tables_ref.at[n], ref, local_sem.at[2 + n])
+        for n, ref in enumerate((right_ref, right_t_ref, left_ref, left_t_ref))
+    ]
+    for fetch in fetches:
+        fetch.start()
     greet(me)
     mail = Mail(send_sem, recv_sem)
     h = me.half
@@ -409,7 +415,7 @@
             for start, v in zip(starts, results):
                 term[pl.ds(start, 2 * GRID), :] = v
 
-    finish = gather(me, mail, res_ref, blk_ref, rfull, sfull, local_sem, forward)
+    finish = gather(me, mail, res_ref, blk_ref, rfull, sfull, local_sem, fetches, forward)
 
     def wave_sq(index):
         signed = jnp.minimum(index, GRID - index).astype(jnp.float32) * (2.0 * math.pi / GRID)
@@ -435,15 +441,14 @@
         Sum(me, mail, term, near_s.at[n], far_s.at[n], near_f.at[n], far_f.at[n], half, first)
         for n, (half, first) in enumerate(((1 - h, "z"), (h, "y")))
     ]
-    order = (2, 1, -1, 0)
-
     def pieces(s, f, off):
         return [me.piece(s.half, **s.off(f, off))]
 
-    for f in order:
+    def far(f):
         backward([p for s in sums for p in pieces(s, f, 2)])
         for s in sums:
             s.far_column(f)
+
     def near(f):
         backward([p for s in sums for e in (1, -1) for p in pieces(s, f, e)])
         for s in sums:
@@ -459,7 +464,10 @@
             elif f:
                 s.near_row(f)
 
-    for step, f in ((near, 2), (near, 1), (near, -1), (own, 2), (near, 0), (own, 1), (own, -1), (own, 0)):
+    for step, f in (
+        (far, 2), (far, 1), (far, -1), (near, 2), (far, 0), (near, 1), (near, -1), (own, 2),
+        (near, 0), (own, 1), (own, -1), (own, 0),
+    ):
         step(f)
     sums[0].own_row()
     swap = mail.send(planes(term, me.piece(1 - h)), out_ref.at[h], me.device(dx=2))
@@ -498,7 +506,7 @@
         high, low = parts(t)
         return np.block([[high, high], [low, np.zeros_like(low)]])
 
-    return [jnp.asarray(t) for t in (right(b), right(b.T), left(b), left(b.T))]
+    return jnp.asarray(np.stack([right(b), right(b.T), left(b), left(b.T)]))
 
 
 def per_device(resident, blocks, occupation):
@@ -508,9 +516,10 @@
     out = pl.pallas_call(
         kernel,
         out_shape=jax.ShapeDtypeStruct((2, ROWS, GRID), jnp.float32),
-        in_specs=[hbm, hbm, pl.BlockSpec(memory_space=pltpu.SMEM)] + [vmem] * 4,
+        in_specs=[hbm, hbm, pl.BlockSpec(memory_space=pltpu.SMEM), hbm],
         out_specs=vmem,
         scratch_shapes=[
+            *[pltpu.VMEM((2 * GRID, 2 * GRID), jnp.bfloat16)] * 4,
             full,
             full,
             full,
@@ -521,7 +530,7 @@
             pltpu.VMEM((2, 2, HALF, GRID), jnp.float32),
             pltpu.SemaphoreType.DMA((MESSAGES,)),
             pltpu.SemaphoreType.DMA((MESSAGES,)),
-            pltpu.SemaphoreType.DMA((2,)),
+            pltpu.SemaphoreType.DMA((6,)),
         ],
         compiler_params=pltpu.CompilerParams(
             collective_id=0, has_side_effects=True, vmem_limit_bytes=56 * 2**20
@@ -532,7 +541,7 @@
         resident.reshape(2, ROWS, GRID),
         blocks.reshape(4, ROWS, GRID),
         occupation,
-        *tables(),
+        tables(),
     )
     return out.reshape(2, PLANES, GRID, GRID)
 

time: 142 us -> 141 us (level)
  no operation moved by 1% of the time
where the time goes in v4:
time: 141 us; the launch traced here: 139 us
  Pallas kernels  138 us (98%)
  local copies, waits for them, and re-layouts  1.87 us (1%)
    pallas_call x1, Pallas kernels, per_device(): pl.pallas_call(kernel, out_shape=jax.ShapeDtypeStruct((2, ROWS, GRID), jn...  138 us

profile of v4, /device:TPU:6, one launch (start us, length us, event | category | flops | bytes accessed | tf_op | source)
XLA Modules:
  0.0 139.4 jit_solution(17684052541120417467)
XLA Ops:
  0.0 137.6 %exchange.1 = f32[2,512,128]{2,1,0:T(8,128)} custom-call(f32[2,512,128]{2,1,0:T(8,128)} %bitcast.5, f32[4,512,128]{2,1,0:T(8,128)} %bitcast.4, f32[16]{0:T(128)} %occ_ref.1, bf16[4,256,256]{2,1,0:T(8,128)(2,1)} %constant.2.clone.tables_ref), custom_call_target="tpu_custom_call" | custom-call | flops 12999999488 | bytes 10000000 | tf_op jit(solution)/shard_map/exchange/pallas_call | solution.py:516
  137.6 1.9 %copy.6 = f32[2,4,128,128]{3,2,1,0:T(8,128)} copy(f32[2,4,128,128]{3,2,1,0:T(8,128)} %bitcast.3) | data formatting | bytes 1048576

commit v5 on v4

--- a/solution.py
+++ b/solution.py
@@ -194,6 +194,7 @@
         core = 1 - me.core if flip else me.core
         return (x // 2) * 16 + align_z(me, x, core) * 4 + (me.y + t) % 4
 
+    swap = mail.send(res_ref.at[1 - h], planes(rfull, mine), me.device(dx=2))
     order = (0, 1, 3, 2)
     align_no = {}
     for t in order:
@@ -220,7 +221,6 @@
             def _():
                 pltpu.make_async_copy(src, dst, local_sem.at[1]).start()
             zero = (remote, src, dst)
-    swap = mail.send(res_ref.at[1 - h], planes(rfull, mine), me.device(dx=2))
     tree_a = Tree(me, mail, rfull, h, "y")
     tree_b = Tree(me, mail, rfull, 1 - h, "z")
     tree_a.start(res_ref.at[h])

time: 141 us -> 138 us (0.979)
  Pallas kernels: 138 us -> 136 us
    pallas_call x1, Pallas kernels: 138 us -> 136 us  [per_device(): pl.pallas_call(kernel, out_shape=jax.ShapeDtypeStruct((2, ROWS, GRID), jn...]
where the time goes in v5:
time: 138 us
  Pallas kernels  136 us (99%)
  local copies, waits for them, and re-layouts  1.87 us (1%)
    pallas_call x1, Pallas kernels, per_device(): pl.pallas_call(kernel, out_shape=jax.ShapeDtypeStruct((2, ROWS, GRID), jn...  136 us

profile of v5, /device:TPU:6, one launch (start us, length us, event | category | flops | bytes accessed | tf_op | source)
XLA Modules:
  0.0 137.6 jit_solution(16631632404259148252)
XLA Ops:
  0.0 135.7 %exchange.1 = f32[2,512,128]{2,1,0:T(8,128)} custom-call(f32[2,512,128]{2,1,0:T(8,128)} %bitcast.5, f32[4,512,128]{2,1,0:T(8,128)} %bitcast.4, f32[16]{0:T(128)} %occ_ref.1, bf16[4,256,256]{2,1,0:T(8,128)(2,1)} %constant.2.clone.tables_ref), custom_call_target="tpu_custom_call" | custom-call | flops 12999999488 | bytes 10000000 | tf_op jit(solution)/shard_map/exchange/pallas_call | solution.py:516
  135.7 1.9 %copy.6 = f32[2,4,128,128]{3,2,1,0:T(8,128)} copy(f32[2,4,128,128]{3,2,1,0:T(8,128)} %bitcast.3) | data formatting | bytes 1048576

commit v6 on v5

--- a/solution.py
+++ b/solution.py
@@ -17,7 +17,7 @@
 KAPPA_SQ = 0.01
 STEPS = ('s0', 'row', 'c0', 's1', 'far', 'c1', 's2', 'c2', 'own', 'early', 'last')
 PITCH = GRID + 8
-DEEP = 16
+DEEP = 32
 
 
 class Place:
@@ -249,9 +249,11 @@
                     pltpu.make_async_copy(zero[1], zero[2], local_sem.at[1]).wait()
             for d in (1, -1):
                 xs[("x", d, back)] = mail.send(dst, dst, me.device(dx=d))
-            xs[("c", 0, back)] = mail.send(dst, dst, me.device(flip=True))
 
     def beside():
+        for t in backs:
+            ref = planes(sfull, spiece(0, False, t))
+            xs[("c", 0, t)] = mail.send(ref, ref, me.device(flip=True))
         for t in backs:
             for d in (1, -1):
                 ref = planes(sfull, spiece(-d, False, t))

time: 138 us -> 137 us (level)
  no operation moved by 1% of the time
where the time goes in v6:
time: 137 us
  Pallas kernels  135 us (99%)
  local copies, waits for them, and re-layouts  1.87 us (1%)
    pallas_call x1, Pallas kernels, per_device(): pl.pallas_call(kernel, out_shape=jax.ShapeDtypeStruct((2, ROWS, GRID), jn...  135 us

profile of v6, /device:TPU:6, one launch (start us, length us, event | category | flops | bytes accessed | tf_op | source)
XLA Modules:
  0.0 137.0 jit_solution(13516163356179512230)
XLA Ops:
  0.0 135.1 %exchange.1 = f32[2,512,128]{2,1,0:T(8,128)} custom-call(f32[2,512,128]{2,1,0:T(8,128)} %bitcast.5, f32[4,512,128]{2,1,0:T(8,128)} %bitcast.4, f32[16]{0:T(128)} %occ_ref.1, bf16[4,256,256]{2,1,0:T(8,128)(2,1)} %constant.2.clone.tables_ref), custom_call_target="tpu_custom_call" | custom-call | flops 12999999488 | bytes 10000000 | tf_op jit(solution)/shard_map/exchange/pallas_call | solution.py:518
  135.1 1.9 %copy.6 = f32[2,4,128,128]{3,2,1,0:T(8,128)} copy(f32[2,4,128,128]{3,2,1,0:T(8,128)} %bitcast.3) | data formatting | bytes 1048576
